TPU v7x, 256 devices: a whole 4x4x8 slice. The times are simulated.
256 devices in a mesh: seq: 8 (over x, core), exp: 32 (over y, z).
Axes of the slice: x: 4, y: 4, z: 8, core: 2. Of those that a mesh axis runs over, the one named last changes fastest.
Arguments:
- heads_primal: bfloat16 [32768, 1280], P('exp', 'seq'), may hold values from -6 to 6
- heads_tangent: bfloat16 [32768, 1280], P('exp', 'seq'), may hold values from -6 to 6
- expert_ids: int32 [32768, 2], P(('exp', 'seq')), may hold values from 0 to 15, all different within a row; in each aligned block of 128 rows (0 to 127, 128 to 255, ...) at most 18 rows name the same one
- gate_weights: float32 [32768, 2], P(('exp', 'seq')), may hold values from 0.2 to 1
- gate_tangent: float32 [32768, 2], P(('exp', 'seq')), may hold values from -1 to 1
- w_gate: bfloat16 [32, 1280, 1536], P('exp'), may hold values from -0.15625 to 0.15625
- w_up: bfloat16 [32, 1280, 1536], P('exp'), may hold values from -0.15625 to 0.15625
- w_down: bfloat16 [32, 1536, 1280], P('exp'), may hold values from -0.109375 to 0.109375
Outputs:
- moe_out: bfloat16 [32768, 1280], P(('exp', 'seq'))
- moe_tangent: bfloat16 [32768, 1280], P(('exp', 'seq'))
Inputs may be any that keep to these rules, and one draw needn't show every extreme that they name: `expert_ids`: each token names two different experts; in the rows of one device (aligned blocks of 128 tokens) no expert is named more than 18 times.
All inputs are finite; a program needn't handle non-finite values.
Results may differ from a plain program's by a relative error of at most 0.0065.
Values may be sent and summed in bfloat16 or wider, within the bound.
A program may use at most 64 MiB of HBM per device.

v0:
```python
import jax
import jax.numpy as jnp
from jax import lax
from jax.sharding import PartitionSpec as P


def expert_half(rows, tans, gate_w, up_w, down_w):
    width = rows.shape[-1]
    lead = rows.shape[:-1]
    both = jnp.concatenate([rows.reshape(-1, width), tans.reshape(-1, width)], 0)
    count = both.shape[0] // 2
    gate_all = jnp.dot(both, gate_w, preferred_element_type=jnp.float32)
    up_all = jnp.dot(both, up_w, preferred_element_type=jnp.float32)
    pre_gate = gate_all[:count]
    tan_gate = gate_all[count:]
    pre_up = up_all[:count]
    tan_up = up_all[count:]
    sigma = jax.nn.sigmoid(pre_gate)
    swish = pre_gate * sigma
    hidden = (swish * pre_up).astype(jnp.bfloat16)
    slope = sigma * (1.0 + pre_gate * (1.0 - sigma))
    hidden_tan = (slope * tan_gate * pre_up + swish * tan_up).astype(jnp.bfloat16)
    parts = jnp.dot(
        jnp.concatenate([hidden, hidden_tan], 0), down_w, preferred_element_type=jnp.float32
    ).astype(jnp.bfloat16)
    return (parts[:count].reshape(lead + (width,)), parts[count:].reshape(lead + (width,)))


def per_device(
    heads_primal, heads_tangent, expert_ids, gate_weights, gate_tangent, w_gate, w_up, w_down
):
    token_p, token_t = (
        lax.all_to_all(heads_primal, "seq", split_axis=0, concat_axis=1, tiled=True),
        lax.all_to_all(heads_tangent, "seq", split_axis=0, concat_axis=1, tiled=True),
    )
    tok_rows = token_p.shape[0]
    width = token_p.shape[1]
    experts = lax.axis_size("exp") // 2
    capacity = tok_rows * 2 * 9 // (8 * experts)
    gate_w = w_gate[0]
    up_w = w_up[0]
    down_w = w_down[0]
    flat_ids = expert_ids.reshape(-1)
    onehot = (flat_ids[:, None] == jnp.arange(experts, dtype=jnp.int32)[None, :]).astype(jnp.int32)
    slot = jnp.sum((jnp.cumsum(onehot, axis=0) - 1) * onehot, axis=1)
    position = flat_ids * capacity + slot
    buf_p = (
        jnp.zeros((experts * capacity, width), jnp.bfloat16)
        .at[position]
        .set(jnp.repeat(token_p, 2, axis=0))
    )
    buf_t = (
        jnp.zeros((experts * capacity, width), jnp.bfloat16)
        .at[position]
        .set(jnp.repeat(token_t, 2, axis=0))
    )
    send_p = jnp.broadcast_to(
        buf_p.reshape(experts, 1, capacity, width), (experts, 2, capacity, width)
    ).reshape(2 * experts, capacity, width)
    send_t = jnp.broadcast_to(
        buf_t.reshape(experts, 1, capacity, width), (experts, 2, capacity, width)
    ).reshape(2 * experts, capacity, width)
    part_p, part_t = expert_half(
        lax.all_to_all(send_p, "exp", split_axis=0, concat_axis=0, tiled=True),
        lax.all_to_all(send_t, "exp", split_axis=0, concat_axis=0, tiled=True),
        gate_w,
        up_w,
        down_w,
    )
    back_p = lax.all_to_all(part_p, "exp", split_axis=0, concat_axis=0, tiled=True)
    back_t = lax.all_to_all(part_t, "exp", split_axis=0, concat_axis=0, tiled=True)
    out_p = (
        back_p.reshape(experts, 2, capacity, width)
        .astype(jnp.float32)
        .sum(axis=1)
        .astype(jnp.bfloat16)
        .reshape(experts * capacity, width)
    )
    out_t = (
        back_t.reshape(experts, 2, capacity, width)
        .astype(jnp.float32)
        .sum(axis=1)
        .astype(jnp.bfloat16)
        .reshape(experts * capacity, width)
    )
    picked_p = out_p[position].astype(jnp.float32).reshape(tok_rows, 2, width)
    picked_t = out_t[position].astype(jnp.float32).reshape(tok_rows, 2, width)
    weight = gate_weights[:, :, None]
    slope_w = gate_tangent[:, :, None]
    moe_out = jnp.sum(weight * picked_p, axis=1).astype(jnp.bfloat16)
    moe_tangent = jnp.sum(weight * picked_t + slope_w * picked_p, axis=1).astype(jnp.bfloat16)
    return (moe_out, moe_tangent)


def solution(mesh):
    in_specs = (
        P("exp", "seq"),
        P("exp", "seq"),
        P(("exp", "seq"), None),
        P(("exp", "seq"), None),
        P(("exp", "seq"), None),
        P("exp", None, None),
        P("exp", None, None),
        P("exp", None, None),
    )
    out_specs = (P(("exp", "seq"), None), P(("exp", "seq"), None))
    return jax.shard_map(
        per_device, mesh=mesh, in_specs=in_specs, out_specs=out_specs, check_vma=False
    )
```

profile of v0, /device:TPU:1, one launch (start us, length us, event | category | flops | bytes accessed | tf_op | source)
XLA Modules:
  0.0 285.2 jit_solution(14081892360006442993)
XLA Ops:
  2.4 6.6 %all-to-all-start = ((bf16[8,128,160]{1,2,0:T(8,128)(2,1)}), bf16[8,128,160]{1,2,0:T(8,128)(2,1)S(1)}, u32[]{:S(2)}, u32[]{:S(2)}) async-start(bf16[8,128,160]{1,2,0:T(8,128)(2,1)} %copy_bitcast_fusion.1), calls=%async_computation | async-start | bytes 655360 | tf_op jit(solution)/shard_map/all_to_all | solution.py:33
  11.8 1.8 copy_bitcast_fusion
  13.6 2.5 all-to-all-done
  16.1 4.5 %all-to-all-start.2 = ((bf16[8,128,160]{1,2,0:T(8,128)(2,1)}), bf16[8,128,160]{1,2,0:T(8,128)(2,1)S(1)}, u32[]{:S(2)}, u32[]{:S(2)}) async-start(bf16[8,128,160]{1,2,0:T(8,128)(2,1)} %copy_bitcast_fusion), calls=%async_computation.2 | async-start | bytes 655360 | tf_op jit(solution)/shard_map/all_to_all | solution.py:34
  21.5 1.9 scatter_custom_fusion
  23.6 4.1 %all-to-all-done.2 = bf16[8,128,160]{1,2,0:T(8,128)(2,1)S(1)} async-done(((bf16[8,128,160]{1,2,0:T(8,128)(2,1)}), bf16[8,128,160]{1,2,0:T(8,128)(2,1)S(1)}, u32[]{:S(2)}, u32[]{:S(2)}) %all-to-all-start.2) | async-done | bytes 327712 | tf_op jit(solution)/shard_map/all_to_all | solution.py:34
  29.1 10.4 %all-to-all-start.1 = ((bf16[32,18,1280]{2,1,0:T(8,128)(2,1)}), bf16[32,18,1280]{2,1,0:T(8,128)(2,1)S(1)}, u32[]{:S(2)}, u32[]{:S(2)}) async-start(bf16[32,18,1280]{2,1,0:T(8,128)(2,1)} %bitcast.50), calls=%async_computation.1 | async-start | bytes 3932160 | tf_op jit(solution)/shard_map/all_to_all | solution.py:64
  41.2 3.1 %scatter_custom_fusion.1 = bf16[288,1280]{1,0:T(8,128)(2,1)} fusion(s32[256]{0:T(256)S(1)} %bitcast.55, bf16[256,1280]{1,0:T(8,128)(2,1)} %reshape.151, bf16[]{:T(256)} %constant.7.clone.1), kind=kCustom, calls=%fused_computation.25 | custom fusion | bytes 737792 | tf_op jit(solution)/shard_map/scatter | solution.py:55
  45.6 39.9 %all-to-all-done.1 = bf16[32,18,1280]{2,1,0:T(8,128)(2,1)S(1)} async-done(((bf16[32,18,1280]{2,1,0:T(8,128)(2,1)}), bf16[32,18,1280]{2,1,0:T(8,128)(2,1)S(1)}, u32[]{:S(2)}, u32[]{:S(2)}) %all-to-all-start.1) | async-done | bytes 1474592 | tf_op jit(solution)/shard_map/all_to_all | solution.py:64
  87.0 7.2 %all-to-all-start.3 = ((bf16[32,18,1280]{2,1,0:T(8,128)(2,1)}), bf16[32,18,1280]{2,1,0:T(8,128)(2,1)}, u32[]{:S(2)}, u32[]{:S(2)}) async-start(bf16[32,18,1280]{2,1,0:T(8,128)(2,1)} %bitcast.51), calls=%async_computation.3 | async-start | bytes 3932160 | tf_op jit(solution)/shard_map/all_to_all | solution.py:65
  95.5 2.6 constant_dynamic-update-slice_fusion.1
  98.1 41.8 %all-to-all-done.3 = bf16[32,18,1280]{2,1,0:T(8,128)(2,1)} async-done(((bf16[32,18,1280]{2,1,0:T(8,128)(2,1)}), bf16[32,18,1280]{2,1,0:T(8,128)(2,1)}, u32[]{:S(2)}, u32[]{:S(2)}) %all-to-all-start.3) | async-done | bytes 1474592 | tf_op jit(solution)/shard_map/all_to_all | solution.py:65
  140.0 2.5 reshape.114
  143.7 7.9 %fusion.1 = f32[1152,1536]{1,0:T(8,128)S(1)} fusion(bf16[1152,1280]{1,0:T(8,128)(2,1)} %constant_dynamic-update-slice_fusion, bf16[1,1280,1536]{2,1,0:T(8,128)(2,1)} %param.14), kind=kOutput, calls=%fused_computation.6 | convolution fusion | flops 4529848320 | bytes 13959168 | tf_op jit(solution)/shard_map/dot_general | solution.py:13
  151.6 4.8 %fusion.3 = f32[1152,1536]{1,0:T(8,128)S(1)} fusion(bf16[1152,1280]{1,0:T(8,128)(2,1)S(1)} %copy-done.2, bf16[1,1280,1536]{2,1,0:T(8,128)(2,1)S(1)} %copy-done.5), kind=kOutput, calls=%fused_computation.8 | convolution fusion | flops 4529848320 | bytes 13959168 | tf_op jit(solution)/shard_map/dot_general | solution.py:12
  156.4 2.0 multiply_convert_fusion
  158.5 6.1 %convolution_convert_fusion = bf16[1152,1280]{1,0:T(8,128)(2,1)S(1)} fusion(bf16[1,1536,1280]{2,1,0:T(8,128)(2,1)S(1)} %copy-done.6, bf16[576,1536]{1,0:T(8,128)(2,1)S(1)} %get-tuple-element.5, bf16[576,1536]{1,0:T(8,128)(2,1)S(1)} %get-tuple-element.4), kind=kOutput, calls=%fused_computation.4 | convolution fusion | flops 4538400768 | bytes 10420224 | tf_op jit(solution)/shard_map/dot_general | solution.py:23
  167.4 6.9 %all-to-all-start.5 = ((bf16[32,18,1280]{2,1,0:T(8,128)(2,1)}), bf16[32,18,1280]{2,1,0:T(8,128)(2,1)S(1)}, u32[]{:S(2)}, u32[]{:S(2)}) async-start(bf16[32,18,1280]{2,1,0:T(8,128)(2,1)} %reshape.118), calls=%async_computation.5 | async-start | bytes 3932160 | tf_op jit(solution)/shard_map/all_to_all | solution.py:71
  174.3 3.4 %reshape.115 = bf16[32,18,1280]{2,1,0:T(8,128)(2,1)} reshape(bf16[576,1280]{1,0:T(8,128)(2,1)} %get-tuple-element.7) | data formatting | bytes 2949120 | tf_op jit(solution)/shard_map/reshape | solution.py:26
  177.7 42.6 %all-to-all-done.5 = bf16[32,18,1280]{2,1,0:T(8,128)(2,1)S(1)} async-done(((bf16[32,18,1280]{2,1,0:T(8,128)(2,1)}), bf16[32,18,1280]{2,1,0:T(8,128)(2,1)S(1)}, u32[]{:S(2)}, u32[]{:S(2)}) %all-to-all-start.5) | async-done | bytes 1474592 | tf_op jit(solution)/shard_map/all_to_all | solution.py:71
  220.3 7.2 %all-to-all-start.4 = ((bf16[32,18,1280]{2,1,0:T(8,128)(2,1)}), bf16[32,18,1280]{2,1,0:T(8,128)(2,1)}, u32[]{:S(2)}, u32[]{:S(2)}) async-start(bf16[32,18,1280]{2,1,0:T(8,128)(2,1)} %reshape.115), calls=%async_computation.4 | async-start | bytes 3932160 | tf_op jit(solution)/shard_map/all_to_all | solution.py:70
  230.2 43.1 %all-to-all-done.4 = bf16[32,18,1280]{2,1,0:T(8,128)(2,1)} async-done(((bf16[32,18,1280]{2,1,0:T(8,128)(2,1)}), bf16[32,18,1280]{2,1,0:T(8,128)(2,1)}, u32[]{:S(2)}, u32[]{:S(2)}) %all-to-all-start.4) | async-done | bytes 1474592 | tf_op jit(solution)/shard_map/all_to_all | solution.py:70
  273.3 1.9 bitcast_reduce_fusion.1
  278.4 6.8 %add_reduce_fusion = (bf16[128,1280]{1,0:T(8,128)(2,1)}, bf16[128,1280]{1,0:T(8,128)(2,1)}) fusion(f32[128,2,1280]{2,1,0:T(2,128)} %reshape.121, f32[128,2,1280]{2,1,0:T(2,128)S(1)} %reshape.122, f32[128,2]{1,0:T(8,128)S(1)} %copy.39, f32[128,2]{1,0:T(8,128)S(1)} %copy.30), kind=kLoop, calls=%fused_computation.23 | loop fusion | flops 1638400 | bytes 3278848 | tf_op jit(solution)/shard_map/reduce_sum | solution.py:91
  (52 shorter events, 22.8 us)
Async XLA Ops:
  0.6 1.0 copy-start
  2.4 13.7 %all-to-all-start = ((bf16[8,128,160]{1,2,0:T(8,128)(2,1)}), bf16[8,128,160]{1,2,0:T(8,128)(2,1)S(1)}, u32[]{:S(2)}, u32[]{:S(2)}) async-start(bf16[8,128,160]{1,2,0:T(8,128)(2,1)} %copy_bitcast_fusion.1), calls=%async_computation | async-start | bytes 655360 | tf_op jit(solution)/shard_map/all_to_all | solution.py:33
  16.1 11.6 %all-to-all-start.2 = ((bf16[8,128,160]{1,2,0:T(8,128)(2,1)}), bf16[8,128,160]{1,2,0:T(8,128)(2,1)S(1)}, u32[]{:S(2)}, u32[]{:S(2)}) async-start(bf16[8,128,160]{1,2,0:T(8,128)(2,1)} %copy_bitcast_fusion), calls=%async_computation.2 | async-start | bytes 655360 | tf_op jit(solution)/shard_map/all_to_all | solution.py:34
  29.1 56.4 %all-to-all-start.1 = ((bf16[32,18,1280]{2,1,0:T(8,128)(2,1)}), bf16[32,18,1280]{2,1,0:T(8,128)(2,1)S(1)}, u32[]{:S(2)}, u32[]{:S(2)}) async-start(bf16[32,18,1280]{2,1,0:T(8,128)(2,1)} %bitcast.50), calls=%async_computation.1 | async-start | bytes 3932160 | tf_op jit(solution)/shard_map/all_to_all | solution.py:64
  87.0 53.0 %all-to-all-start.3 = ((bf16[32,18,1280]{2,1,0:T(8,128)(2,1)}), bf16[32,18,1280]{2,1,0:T(8,128)(2,1)}, u32[]{:S(2)}, u32[]{:S(2)}) async-start(bf16[32,18,1280]{2,1,0:T(8,128)(2,1)} %bitcast.51), calls=%async_computation.3 | async-start | bytes 3932160 | tf_op jit(solution)/shard_map/all_to_all | solution.py:65
  143.7 7.9 %copy-start.2 = (bf16[1152,1280]{1,0:T(8,128)(2,1)S(1)}, bf16[1152,1280]{1,0:T(8,128)(2,1)}, u32[]{:S(2)}) copy-start(bf16[1152,1280]{1,0:T(8,128)(2,1)} %constant_dynamic-update-slice_fusion) | copy-start | bytes 8847364
  143.7 8.0 %copy-start.5 = (bf16[1,1280,1536]{2,1,0:T(8,128)(2,1)S(1)}, bf16[1,1280,1536]{2,1,0:T(8,128)(2,1)}, u32[]{:S(2)}) copy-start(bf16[1,1280,1536]{2,1,0:T(8,128)(2,1)} %param.13) | copy-start | bytes 11796484
  156.4 2.1 copy-start.6
  167.4 52.9 %all-to-all-start.5 = ((bf16[32,18,1280]{2,1,0:T(8,128)(2,1)}), bf16[32,18,1280]{2,1,0:T(8,128)(2,1)S(1)}, u32[]{:S(2)}, u32[]{:S(2)}) async-start(bf16[32,18,1280]{2,1,0:T(8,128)(2,1)} %reshape.118), calls=%async_computation.5 | async-start | bytes 3932160 | tf_op jit(solution)/shard_map/all_to_all | solution.py:71
  174.3 53.2 %copy-start.3 = (f32[128,2]{0,1:T(2,128)S(1)}, f32[128,2]{0,1:T(2,128)}, u32[]{:S(2)}) copy-start(f32[128,2]{0,1:T(2,128)} %param.11) | copy-start | bytes 3076
  174.3 53.3 %copy-start.4 = (f32[128,2]{0,1:T(2,128)S(1)}, f32[128,2]{0,1:T(2,128)}, u32[]{:S(2)}) copy-start(f32[128,2]{0,1:T(2,128)} %param.12) | copy-start | bytes 3076
  220.3 53.0 %all-to-all-start.4 = ((bf16[32,18,1280]{2,1,0:T(8,128)(2,1)}), bf16[32,18,1280]{2,1,0:T(8,128)(2,1)}, u32[]{:S(2)}, u32[]{:S(2)}) async-start(bf16[32,18,1280]{2,1,0:T(8,128)(2,1)} %reshape.115), calls=%async_computation.4 | async-start | bytes 3932160 | tf_op jit(solution)/shard_map/all_to_all | solution.py:70
  275.4 9.8 %copy-start.1 = (bf16[1024,160]{0,1:T(8,128)(2,1)S(1)}, bf16[1024,160]{0,1:T(8,128)(2,1)}, u32[]{:S(2)}) copy-start(bf16[1024,160]{0,1:T(8,128)(2,1)} %param.8) | copy-start | bytes 983044
where the time goes:
time: 287 us; the launch traced here: 285 us
  waiting for transfers between devices  174 us (61%)
  starting transfers between devices  42.7 us (15%)
  local copies, waits for them, and re-layouts  36.3 us (13%)
  matrix products  18.8 us (7%)
  other arithmetic  12.4 us (4%)
    all_to_all x1, waiting for transfers between devices, per_device(): lax.all_to_all(part_p, 'exp', split_axis=0, concat_axis=0, tiled=True)  43.1 us
    all_to_all x1, waiting for transfers between devices, per_device(): lax.all_to_all(part_t, 'exp', split_axis=0, concat_axis=0, tiled=True)  42.6 us
    all_to_all x1, waiting for transfers between devices, per_device(): lax.all_to_all(send_t, 'exp', split_axis=0, concat_axis=0, tiled=True)  41.8 us
    all_to_all x1, waiting for transfers between devices, per_device(): lax.all_to_all(send_p, 'exp', split_axis=0, concat_axis=0, tiled=True)  39.9 us
    all_to_all x1, starting transfers between devices, per_device(): lax.all_to_all(send_p, 'exp', split_axis=0, concat_axis=0, tiled=True)  10.4 us
    dot_general x1, matrix products, expert_half(): up_all = jnp.dot(both, up_w, preferred_element_type=jnp.float32)  7.93 us
    all_to_all x1, starting transfers between devices, per_device(): lax.all_to_all(part_p, 'exp', split_axis=0, concat_axis=0, tiled=True)  7.22 us
    all_to_all x1, starting transfers between devices, per_device(): lax.all_to_all(send_t, 'exp', split_axis=0, concat_axis=0, tiled=True)  7.18 us
  transfers between devices with their start and end apart: 6, of which 6 were waited for; matrix products, arithmetic and copies ran while one was open for 8% of the time, Pallas kernels for 0%

commit v1 on v0

v1 whole, which is shorter than its diff:
```python
import functools

import jax
import jax.numpy as jnp
from jax import lax
from jax.experimental import pallas as pl
from jax.experimental.pallas import tpu as pltpu
from jax.sharding import PartitionSpec as P

MESH = pl.DeviceIdType.MESH
BF, F32 = jnp.bfloat16, jnp.float32
HOPS = (0, -1, 2, -3)
LANES = 2944
ROWS = 16


def iota(shape, dim):
    return lax.broadcasted_iota(jnp.int32, shape, dim)


def pack_matrix(n, transposed):
    shape = (ROWS * n, ROWS * n)
    a, b = (iota(shape, 1), iota(shape, 0)) if transposed else (iota(shape, 0), iota(shape, 1))
    k, rho = a >> 4, a & 15
    return (b == (rho >> 1) * (2 * n) + k * 2 + (rho & 1)).astype(BF)


def pack_tail(tail, n, out):
    matrix = pack_matrix(n, False)
    for t in range(3):
        groups = 8 if t < 2 else 4
        stacked = jnp.concatenate([tail[:, 128 * (8 * t + j) : 128 * (8 * t + j + 1)] for j in range(groups)], 0)
        out[:, 2560 + 128 * t : 2560 + 128 * (t + 1)] = jnp.dot(
            matrix[:, : groups * 2 * n], stacked, preferred_element_type=F32
        ).astype(BF)


def unpack_tail(messages, n, out):
    matrix = pack_matrix(n, True)
    for t in range(3):
        groups = 8 if t < 2 else 4
        rows = jnp.dot(
            matrix[: groups * 2 * n], messages[:, 2560 + 128 * t : 2560 + 128 * (t + 1)], preferred_element_type=F32
        ).astype(BF)
        for j in range(groups):
            out[:, 128 * (8 * t + j) : 128 * (8 * t + j + 1)] = rows[2 * n * j : 2 * n * (j + 1)]


def layer(
    hp, ht, ids, gates, slopes, w_gate, w_up, w_down, out_p, out_t,
    cols, toks, sbuf, rcv, rsend, rback, gu_own, dn_own, gu_oth, dn_oth, xin, hid, part, tails, wsel,
    own_sem, rg_sem, tk_sem, rt_sem, z_sem, x_sem, c_sem,
):
    seq, ex = lax.axis_index("seq"), lax.axis_index("exp")
    x, c, y, z = seq // 2, lax.rem(seq, 2), ex // 8, lax.rem(ex, 8)
    sgn = 1 - 2 * lax.rem(z, 2)

    def at(xx, cc, yy, zz):
        return (lax.rem(xx + 8, 4) * 2 + lax.rem(cc + 2, 2), lax.rem(yy + 8, 4) * 8 + lax.rem(zz + 16, 8))

    def dest(k):
        return at(x, c, y + k % 4, z + HOPS[k // 4] * sgn)

    def source(k):
        return at(x, c, y - k % 4, z - (k // 4) * sgn)

    partner = at(x, c, y, z + sgn)
    other_core = at(x, 1 - c, y, z)

    def remote(src, dst, send, recv, device):
        return pltpu.make_async_remote_copy(src, dst, send, recv, device_id=device, device_id_type=MESH)

    barrier = pltpu.get_barrier_semaphore()
    for i in range(1, 8):
        pl.semaphore_signal(barrier, inc=1, device_id=(lax.rem(seq + i, 8), ex), device_id_type=MESH)
    for k in range(1, 16):
        pl.semaphore_signal(barrier, inc=1, device_id=dest(k), device_id_type=MESH)
        pl.semaphore_signal(barrier, inc=1, device_id=source(k), device_id_type=MESH)
    pl.semaphore_signal(barrier, inc=1, device_id=partner, device_id_type=MESH)

    own = [
        pltpu.make_async_copy(w.at[0, :, pl.ds(384 * q, 384)], gu_own.at[q, :, pl.ds(384 * g, 384)], own_sem.at[2 * q + g])
        for q in range(4)
        for g, w in enumerate((w_gate, w_up))
    ]
    own.append(pltpu.make_async_copy(w_down.at[0], dn_own, own_sem.at[8]))
    for copy in own:
        copy.start()
    pl.semaphore_wait(barrier, 38)

    def regroup(i, kind):
        to = lax.rem(seq + i, 8)
        heads = (hp, ht)[kind]
        n = 2 * i + kind
        return remote(
            heads.at[pl.ds(pl.multiple_of(to * 128, 128), 128)], cols.at[seq, kind],
            rg_sem.at[0, n], rg_sem.at[1, n], (to, ex),
        )

    for i in range(1, 8):
        for kind in range(2):
            regroup(i, kind).start()
    mine = pl.ds(pl.multiple_of(seq * 128, 128), 128)
    cols[seq, 0] = hp[mine, :]
    cols[seq, 1] = ht[mine, :]

    def region(g, q, core, mine_too):
        if g == 2:
            rows = pl.ds(pl.multiple_of(q * 384 + core * 192, 64), 192)
            return (w_down.at[0, rows] if mine_too else None), dn_oth.at[rows]
        rows = pl.ds(pl.multiple_of(core * 640, 128), 640)
        lanes = pl.ds(pl.multiple_of(q * 384, 128), 384)
        src = (w_gate, w_up)[g].at[0, rows, lanes] if mine_too else None
        return src, gu_oth.at[q, rows, pl.ds(384 * g, 384)]

    def cross(g):
        src, dst = region(g, x, c, True)
        return remote(src, dst, z_sem.at[0, g], z_sem.at[1, g], partner)

    def over_x(g, i):
        _, ref = region(g, x, c, False)
        return remote(ref, ref, x_sem.at[0, 3 * g + i - 1], x_sem.at[1, 3 * g + i - 1], at(x + i, c, y, z))

    def from_x(g, i):
        _, ref = region(g, lax.rem(x - i + 4, 4), c, False)
        return remote(ref, ref, x_sem.at[0, 3 * g + i - 1], x_sem.at[1, 3 * g + i - 1], at(x + i, c, y, z))

    def over_core(g, i, core):
        _, ref = region(g, lax.rem(x - i + 4, 4), core, False)
        return remote(ref, ref, c_sem.at[0, 4 * g + i], c_sem.at[1, 4 * g + i], other_core)

    for g in range(3):
        cross(g).start()

    def row(ref, k):
        return jnp.broadcast_to(ref[:, k : k + 1].astype(F32), (128, 128)).T[:16]

    k16 = iota((16, 128), 0)
    cls = k16 >> 2
    zk = lax.rem(z + sgn * jnp.where(cls == 0, 0, jnp.where(cls == 1, -1, jnp.where(cls == 2, 2, -3))) + 16, 8)
    named = (4 * lax.rem(y + (k16 & 3), 4) + (zk >> 1)).astype(F32)
    first, second = (row(ids, k) == named for k in range(2))
    member = jnp.logical_or(first, second)
    before = (iota((128, 128), 0) < iota((128, 128), 1)).astype(BF)
    rank = jnp.dot(member.astype(BF), before, preferred_element_type=F32)
    values = [jnp.where(member, rank, -1.0).astype(BF)]
    for ref in (gates, slopes):
        weight = jnp.where(first, row(ref, 0), jnp.where(second, row(ref, 1), 0.0))
        high = weight.astype(BF)
        values += [high, (weight - high.astype(F32)).astype(BF)]
    slot_row = iota((288, 16), 0)
    spread = (jnp.where(slot_row < 256, slot_row >> 4, (slot_row - 256) >> 1) == iota((288, 16), 1)).astype(BF)
    spread = jnp.dot(spread, jnp.concatenate(values, 1), preferred_element_type=F32)
    a = iota((288, 128), 0)
    chosen = spread[:, :128] == jnp.where(a < 256, a & 15, 16 + (a & 1)).astype(F32)
    for i, part_of in enumerate((1, 3, 2, 4)):
        wsel[i // 2, :, 128 * (i % 2) : 128 * (i % 2 + 1)] = jnp.where(
            chosen, spread[:, 128 * part_of : 128 * (part_of + 1)], 0.0
        ).astype(BF)
    chosen = chosen.astype(BF)

    for i in range(1, 8):
        for kind in range(2):
            regroup(i, kind).wait_recv()
    for half in range(2):
        for kind in range(2):
            total = jnp.zeros((128, 640), F32)
            for q in range(4):
                place = (iota((160, 640), 1) == iota((160, 640), 0) + 160 * q).astype(BF)
                total += jnp.dot(cols[4 * half + q, kind], place, preferred_element_type=F32)
            toks[:, 1280 * kind + 640 * half : 1280 * kind + 640 * (half + 1)] = total.astype(BF)
    sbuf[:, :2560] = jnp.dot(chosen[:256], toks[...], preferred_element_type=F32).astype(BF)
    pack_tail(jnp.dot(chosen[256:], toks[...], preferred_element_type=F32).astype(BF), 16, sbuf)

    def rows_of(k):
        return pl.ds(ROWS * k, ROWS)

    def token(k):
        return remote(sbuf.at[rows_of(k)], rcv.at[rows_of(k)], tk_sem.at[0, k], tk_sem.at[1, k], dest(k))

    def give_back(k):
        return remote(rsend.at[rows_of(k)], rback.at[rows_of(k)], rt_sem.at[0, k], rt_sem.at[1, k], source(k))

    for j in range(4):
        for d in (3, 2, 1, 0):
            if d or j:
                token(4 * d + j).start()
    rcv[:ROWS] = sbuf[:ROWS]

    def hidden(b, weights):
        @pl.loop(0, 4)
        def _(q):
            both = jnp.dot(xin[b], weights[q], preferred_element_type=F32)
            pre_gate, tan_gate = both[:144, :384], both[144:, :384]
            pre_up, tan_up = both[:144, 384:], both[144:, 384:]
            sigma = jax.nn.sigmoid(pre_gate)
            swish = pre_gate * sigma
            slope = sigma * (1.0 + pre_gate * (1.0 - sigma))
            lanes = pl.ds(pl.multiple_of(q * 384, 128), 384)
            hid[b, :144, lanes] = (swish * pre_up).astype(BF)
            hid[b, 144:, lanes] = (slope * tan_gate * pre_up + swish * tan_up).astype(BF)

    def arrive(g):
        cross(g).wait_recv()
        for i in (1, 3, 2):
            over_x(g, i).start()
        over_core(g, 0, c).start()

    def pass_on(g):
        for i in (1, 3, 2):
            from_x(g, i).wait_recv()
            over_core(g, i, c).start()

    def own_half(b):
        for k in range(8 * b, 8 * b + 8):
            if k:
                token(k).wait_recv()
        here = rcv.at[128 * b : 128 * (b + 1)]
        unpack_tail(here, 8, tails)
        for kind in range(2):
            xin[b, 144 * kind : 144 * kind + 128] = here[:, 1280 * kind : 1280 * (kind + 1)]
            xin[b, 144 * kind + 128 : 144 * (kind + 1)] = tails[:, 1280 * kind : 1280 * (kind + 1)]
        hidden(b, gu_own)
        part[b] = jnp.dot(hid[b], dn_own[...], preferred_element_type=F32).astype(BF)

    for copy in own:
        copy.wait()
    arrive(0)
    arrive(1)
    pass_on(0)
    arrive(2)
    own_half(0)
    pass_on(1)
    own_half(1)
    for g in range(2):
        for i in range(4):
            over_core(g, i, 1 - c).wait_recv()
    hidden(1, gu_oth)
    hidden(0, gu_oth)
    pass_on(2)
    for i in range(4):
        over_core(2, i, 1 - c).wait_recv()
    for b in (1, 0):
        here = jnp.dot(hid[b], dn_oth[...], preferred_element_type=F32).astype(BF)
        total = (here.astype(F32) + part[b].astype(F32)).astype(BF)
        out = rsend.at[128 * b : 128 * (b + 1)]
        for kind in range(2):
            out[:, 1280 * kind : 1280 * (kind + 1)] = total[144 * kind : 144 * kind + 128]
        pack_tail(jnp.concatenate([total[128:144], total[272:288]], 1), 8, out)
        for k in (15, 14, 13, 12, 11, 10, 9, 8) if b else (7, 6, 5, 4, 3, 2, 1):
            give_back(k).start()
    rback[:ROWS] = rsend[:ROWS]
    for k in range(1, 16):
        give_back(k).wait_recv()

    unpack_tail(rback, 16, toks.at[:32])

    def combine(side, main_lanes, width):
        total = jnp.zeros((width, 1280), F32)
        for i in range(2):
            total += lax.dot_general(
                wsel[i, :256, :width], rback[:, main_lanes], (((0,), (0,)), ((), ())), preferred_element_type=F32
            )
            total += lax.dot_general(
                wsel[i, 256:, :width], toks[:32, main_lanes], (((0,), (0,)), ((), ())), preferred_element_type=F32
            )
        return total

    from_p = combine(0, slice(0, 1280), 256)
    out_p[...] = from_p[:128].astype(BF)
    out_t[...] = (combine(1, slice(1280, 2560), 128) + from_p[128:]).astype(BF)

    for i in range(1, 8):
        for kind in range(2):
            regroup(i, kind).wait_send()
    for k in range(1, 16):
        token(k).wait_send()
        give_back(k).wait_send()
    for g in range(3):
        cross(g).wait_send()
        for i in range(1, 4):
            over_x(g, i).wait_send()
        for i in range(4):
            over_core(g, i, c).wait_send()


def per_device(*args):
    vmem, hbm = pl.BlockSpec(memory_space=pltpu.VMEM), pl.BlockSpec(memory_space=pl.ANY)
    dma = pltpu.SemaphoreType.DMA
    return pl.pallas_call(
        layer,
        out_shape=(jax.ShapeDtypeStruct((128, 1280), BF),) * 2,
        in_specs=[vmem] * 5 + [hbm] * 3,
        out_specs=(vmem, vmem),
        scratch_shapes=[
            pltpu.VMEM((8, 2, 128, 160), BF),
            pltpu.VMEM((128, 2560), BF),
            pltpu.VMEM((256, LANES), BF),
            pltpu.VMEM((256, LANES), BF),
            pltpu.VMEM((256, LANES), BF),
            pltpu.VMEM((256, LANES), BF),
            pltpu.VMEM((4, 1280, 768), BF),
            pltpu.VMEM((1536, 1280), BF),
            pltpu.VMEM((4, 1280, 768), BF),
            pltpu.VMEM((1536, 1280), BF),
            pltpu.VMEM((2, 288, 1280), BF),
            pltpu.VMEM((2, 288, 1536), BF),
            pltpu.VMEM((2, 288, 1280), BF),
            pltpu.VMEM((16, 2560), BF),
            pltpu.VMEM((2, 288, 256), BF),
            dma((9,)),
            dma((2, 16)),
            dma((2, 16)),
            dma((2, 16)),
            dma((2, 3)),
            dma((2, 9)),
            dma((2, 12)),
        ],
        compiler_params=pltpu.CompilerParams(
            collective_id=0, has_side_effects=True, vmem_limit_bytes=60 << 20
        ),
    )(*args)


def solution(mesh):
    tokens = P(("exp", "seq"), None)
    halves = P("exp", None, None)
    return jax.shard_map(
        per_device,
        mesh=mesh,
        in_specs=(P("exp", "seq"), P("exp", "seq"), tokens, tokens, tokens, halves, halves, halves),
        out_specs=(tokens, tokens),
        check_vma=False,
    )
```

time: 287 us -> 145 us (0.51)
  waiting for transfers between devices: 174 us -> 0 us
  Pallas kernels: 0 us -> 133 us
  starting transfers between devices: 42.7 us -> 0 us
  local copies, waits for them, and re-layouts: 36.3 us -> 11.6 us
  matrix products: 18.8 us -> 0 us
  other arithmetic: 12.4 us -> 0 us
    all_to_all x6 -> x0, waiting for transfers between devices: 174 us -> none  [the longest x1 43.1 us: per_device(): lax.all_to_all(part_p, 'exp', split_axis=0, concat_axis=0, tiled=True)]
    pallas_call x0 -> x1, Pallas kernels: none -> 133 us  [per_device(): pl.pallas_call(layer, out_shape=(jax.ShapeDtypeStruct((128, 1280), BF),)...]
    all_to_all x6 -> x0, starting transfers between devices: 42.7 us -> none  [the longest x1 10.4 us: per_device(): lax.all_to_all(send_p, 'exp', split_axis=0, concat_axis=0, tiled=True)]
    dot_general x3 -> x0, matrix products: 18.8 us -> none  [the longest x1 7.93 us: expert_half(): up_all = jnp.dot(both, up_w, preferred_element_type=jnp.float32)]
    reshape x8 -> x0, local copies, waits for them, and re-layouts: 10.5 us -> none  [the longest x1 3.39 us: expert_half(): parts[:count].reshape(lead + (width,))]
    reduce_sum x4 -> x0, other arithmetic: 9.07 us -> none  [the longest x1 6.79 us: per_device(): jnp.sum(weight * picked_t + slope_w * picked_p, axis=1).astype(jnp.bfloat16)]
    unnamed x18 -> x7, local copies, waits for them, and re-layouts: 4.74 us -> 11.6 us
    broadcast_in_dim x6 -> x0, local copies, waits for them, and re-layouts: 5.08 us -> none  [the longest x2 2.78 us: per_device(): jnp.broadcast_to(buf_t.reshape(experts, 1, capacity, width), (experts, 2,...]
  transfers between devices with their start and end apart: 6 -> 0, of which waited for: 6 -> 0; matrix products, arithmetic and copies ran while one was open for 8% -> 0% of each run, Pallas kernels for 0% -> 0%
where the time goes in v1:
time: 145 us
  Pallas kernels  133 us (92%)
  local copies, waits for them, and re-layouts  11.6 us (8%)
    pallas_call x1, Pallas kernels, per_device(): pl.pallas_call(layer, out_shape=(jax.ShapeDtypeStruct((128, 1280), BF),)...  133 us
    unnamed x7, local copies, waits for them, and re-layouts  11.6 us

profile of v1, /device:TPU:1, one launch (start us, length us, event | category | flops | bytes accessed | tf_op | source)
XLA Modules:
  0.0 145.2 jit_solution(2795346307183026217)
XLA Ops:
  0.6 1.4 copy.12.ids
  2.0 1.4 copy.13.gates
  3.5 1.4 copy.14.slopes
  4.9 2.0 %copy.10.hp = bf16[1024,160]{1,0:T(8,128)(2,1)} copy(bf16[1024,160]{0,1:T(8,128)(2,1)} %param.8) | data formatting | bytes 655360 | tf_op args[0]
  6.8 2.0 %copy.11.ht = bf16[1024,160]{1,0:T(8,128)(2,1)} copy(bf16[1024,160]{0,1:T(8,128)(2,1)} %param.9) | data formatting | bytes 655360 | tf_op args[1]
  8.8 132.9 %shard_map.95 = (bf16[128,1280]{1,0:T(8,128)(2,1)}, bf16[128,1280]{1,0:T(8,128)(2,1)}) custom-call(bf16[1024,160]{1,0:T(8,128)(2,1)} %copy.10.hp, bf16[1024,160]{1,0:T(8,128)(2,1)} %copy.11.ht, s32[128,2]{1,0:T(8,128)} %copy.12.ids, f32[128,2]{1,0:T(8,128)} %copy.13.gates, f32[128,2]{1,0:T(8,128)} %copy.14.slopes, bf16[1,1280,1536]{2,1,0:T(8,128)(2,1)} %w_gate.1, ...), custom_call_target="tpu_custom_call" | custom-call | tf_op jit(solution)/shard_map/pallas_call | solution.py:290
  141.7 1.7 %copy.17 = bf16[128,1280]{1,0:T(8,128)(2,1)} copy(bf16[128,1280]{1,0:T(8,128)(2,1)} %get-tuple-element.4) | data formatting | bytes 655360
  143.5 1.7 %copy.18 = bf16[128,1280]{1,0:T(8,128)(2,1)} copy(bf16[128,1280]{1,0:T(8,128)(2,1)} %get-tuple-element.5) | data formatting | bytes 655360

commit v2 on v1

v2 whole, which is shorter than its diff:
```python
import functools

import jax
import jax.numpy as jnp
from jax import lax
from jax.experimental import pallas as pl
from jax.experimental.pallas import tpu as pltpu
from jax.sharding import PartitionSpec as P

MESH = pl.DeviceIdType.MESH
BF, F32 = jnp.bfloat16, jnp.float32
HOPS = (0, -1, 2, -3)
LANES = 2944
ROWS = 16
CHUNKS = 6


def iota(shape, dim):
    return lax.broadcasted_iota(jnp.int32, shape, dim)


def pack_matrix(n, transposed):
    shape = (ROWS * n, ROWS * n)
    a, b = (iota(shape, 1), iota(shape, 0)) if transposed else (iota(shape, 0), iota(shape, 1))
    k, rho = a >> 4, a & 15
    return (b == (rho >> 1) * (2 * n) + k * 2 + (rho & 1)).astype(BF)


def pack_tail(tail, n, out):
    matrix = pack_matrix(n, False)
    for t in range(3):
        groups = 8 if t < 2 else 4
        stacked = jnp.concatenate([tail[:, 128 * (8 * t + j) : 128 * (8 * t + j + 1)] for j in range(groups)], 0)
        out[:, 2560 + 128 * t : 2560 + 128 * (t + 1)] = jnp.dot(
            matrix[:, : groups * 2 * n], stacked, preferred_element_type=F32
        ).astype(BF)


def unpack_tail(messages, n, out):
    matrix = pack_matrix(n, True)
    for t in range(3):
        groups = 8 if t < 2 else 4
        rows = jnp.dot(
            matrix[: groups * 2 * n], messages[:, 2560 + 128 * t : 2560 + 128 * (t + 1)], preferred_element_type=F32
        ).astype(BF)
        for j in range(groups):
            out[:, 128 * (8 * t + j) : 128 * (8 * t + j + 1)] = rows[2 * n * j : 2 * n * (j + 1)]


def layer(
    hp, ht, ids, gates, slopes, w_gate, w_up, w_down, out,
    toks, sbuf, rcv, rsend, rback, gu_own, dn_own, gu_oth, dn_oth, xin, hid, part, tails, wsel,
    own_sem, rg_sem, tk_sem, rt_sem, z_sem, x_sem, r_sem, c_sem, plane_sem,
):
    seq, ex = lax.axis_index("seq"), lax.axis_index("exp")
    x, c, y, z = seq // 2, lax.rem(seq, 2), ex // 8, lax.rem(ex, 8)
    sgn = 1 - 2 * lax.rem(z, 2)

    ys = [lax.rem(y + j, 4) * 8 for j in range(4)]
    around = [lax.rem(z + 8 + hop * sgn, 8) for hop in (0, 1, 2, -1, -2, -3)]
    xs = [lax.rem(x + i, 4) for i in range(4)]

    def dest(k):
        return (seq, ys[k % 4] + around[(0, 3, 2, 5)[k // 4]])

    def source(k):
        return (seq, ys[-k % 4] + around[(0, 3, 4, 5)[k // 4]])

    partner = (seq, ys[0] + around[1])
    other_core = (2 * x + 1 - c, ex)

    def remote(src, dst, send, recv, device):
        return pltpu.make_async_remote_copy(src, dst, send, recv, device_id=device, device_id_type=MESH)

    barrier = pltpu.get_barrier_semaphore()
    for i in range(1, 8):
        pl.semaphore_signal(barrier, inc=1, device_id=(lax.rem(seq + i, 8), ex), device_id_type=MESH)
    for i in range(1, 8):
        pl.semaphore_signal(barrier, inc=1, device_id=(seq, ys[0] + lax.rem(z + i, 8)), device_id_type=MESH)
    for j in range(1, 4):
        pl.semaphore_signal(barrier, inc=1, device_id=(seq, ys[j] + z), device_id_type=MESH)

    own = [
        pltpu.make_async_copy(w.at[0, :, pl.ds(384 * q, 384)], gu_own.at[q, :, pl.ds(384 * g, 384)], own_sem.at[2 * q + g])
        for q in range(4)
        for g, w in enumerate((w_gate, w_up))
    ]
    own.append(pltpu.make_async_copy(w_down.at[0], dn_own, own_sem.at[8]))
    pl.semaphore_wait(barrier, 17)

    def regroup(i, kind):
        to = lax.rem(seq + i, 8)
        n = 2 * i + kind
        src = (hp, ht)[kind].at[:, pl.ds(pl.multiple_of(to * 128, 128), 128)]
        dst = toks.at[kind, pl.ds(pl.multiple_of(seq * 160, 32), 160)]
        if i == 0:
            return pltpu.make_async_copy(src, dst, rg_sem.at[1, n])
        return remote(src, dst, rg_sem.at[0, n], rg_sem.at[1, n], (to, ex))

    for kind in range(2):
        for i in range(8):
            regroup(i, kind).start()

    def region(n, q, core, half=None, source=False):
        g, sub = n // 2, n % 2
        size = 320 if g < 2 else 96
        first = core * (2 * size) + sub * size
        if half is not None:
            size //= 2
            first += half * size
        if g == 2:
            rows = pl.ds(pl.multiple_of(q * 384 + first, 16), size)
            return w_down.at[0, rows] if source else dn_oth.at[rows]
        rows = pl.ds(pl.multiple_of(first, 16), size)
        if source:
            return (w_gate, w_up)[g].at[0, rows, pl.ds(pl.multiple_of(q * 384, 128), 384)]
        return gu_oth.at[q, rows, pl.ds(384 * g, 384)]

    def cross(n):
        return remote(region(n, x, c, source=True), region(n, x, c), z_sem.at[0, n], z_sem.at[1, n], partner)

    def along(ref, sems, n, step):
        i = 2 * n + (step < 0)
        return remote(ref, ref, sems.at[0, i], sems.at[1, i], (2 * xs[step % 4] + c, ex))

    def send_x(n, step):
        return along(region(n, x, c), x_sem, n, step)

    def recv_x(n, step):
        return along(region(n, xs[-step % 4], c), x_sem, n, step)

    def send_on(n, step):
        return along(region(n, xs[-step % 4], c, half=int(step < 0)), r_sem, n, step)

    def recv_on(n, step):
        return along(region(n, xs[2], c, half=int(step < 0)), r_sem, n, step)

    def over_core(n, i, core):
        ref = region(n, xs[(0, 3, 1, 2)[i]], core)
        return remote(ref, ref, c_sem.at[0, 4 * n + i], c_sem.at[1, 4 * n + i], other_core)

    for n in range(CHUNKS):
        cross(n).start()
    for j in range(1, 4):
        pl.semaphore_signal(plane_sem, inc=1, device_id=(seq, ys[j] + z), device_id_type=MESH)
    for copy in own:
        copy.start()

    def row(ref, k):
        return jnp.broadcast_to(ref[k : k + 1, :].astype(F32), (16, 128))

    k16 = iota((16, 128), 0)
    cls = k16 >> 2
    zk = lax.rem(z + sgn * jnp.where(cls == 0, 0, jnp.where(cls == 1, -1, jnp.where(cls == 2, 2, -3))) + 16, 8)
    named = (4 * lax.rem(y + (k16 & 3), 4) + (zk >> 1)).astype(F32)
    first, second = (row(ids, k) == named for k in range(2))
    member = jnp.logical_or(first, second)
    before = (iota((128, 128), 0) < iota((128, 128), 1)).astype(BF)
    rank = jnp.dot(member.astype(BF), before, preferred_element_type=F32)
    values = [jnp.where(member, rank, -1.0).astype(BF)]
    for ref in (gates, slopes):
        weight = jnp.where(first, row(ref, 0), jnp.where(second, row(ref, 1), 0.0))
        high = weight.astype(BF)
        values += [high, (weight - high.astype(F32)).astype(BF)]
    slot_row = iota((288, 16), 0)
    spread = (jnp.where(slot_row < 256, slot_row >> 4, (slot_row - 256) >> 1) == iota((288, 16), 1)).astype(BF)
    spread = jnp.dot(spread, jnp.concatenate(values, 1), preferred_element_type=F32)
    a = iota((288, 128), 0)
    chosen = spread[:, :128] == jnp.where(a < 256, a & 15, 16 + (a & 1)).astype(F32)
    for i, part_of in enumerate((1, 3, 2, 4)):
        wsel[i // 2, :, 128 * (i % 2) : 128 * (i % 2 + 1)] = jnp.where(
            chosen, spread[:, 128 * part_of : 128 * (part_of + 1)], 0.0
        ).astype(BF)
    chosen = chosen.astype(BF)

    def arrive(n):
        cross(n).wait_recv()
        for step in (1, -1):
            send_x(n, step).start()
        over_core(n, 0, c).start()

    def pass_on(n):
        for i, step in ((1, 1), (2, -1)):
            recv_x(n, step).wait_recv()
            send_on(n, step).start()
            over_core(n, i, c).start()

    def finish(n):
        for step in (1, -1):
            recv_on(n, step).wait_recv()
        over_core(n, 3, c).start()

    arrive(0)
    for kind in range(2):
        regroup(0, kind).wait()
        for i in range(1, 8):
            regroup(i, kind).wait_recv()

    def dispatch(rows, kind):
        return lax.dot_general(
            rows, toks[kind], (((1,), (1,)), ((), ())), preferred_element_type=F32
        ).astype(BF)

    for kind in range(2):
        sbuf[:, 1280 * kind : 1280 * (kind + 1)] = dispatch(chosen[:256], kind)
    pack_tail(jnp.concatenate([dispatch(chosen[256:], kind) for kind in range(2)], 1), 16, sbuf)

    def rows_of(k):
        return pl.ds(ROWS * k, ROWS)

    def token(k):
        return remote(sbuf.at[rows_of(k)], rcv.at[rows_of(k)], tk_sem.at[0, k], tk_sem.at[1, k], dest(k))

    def give_back(k):
        return remote(rsend.at[rows_of(k)], rback.at[rows_of(k)], rt_sem.at[0, k], rt_sem.at[1, k], source(k))

    pl.semaphore_wait(plane_sem, 3)
    for first in (0, 2):
        for j in range(4):
            for d in (first + 1, first):
                if d or j:
                    token(4 * d + j).start()
    rcv[:ROWS] = sbuf[:ROWS]

    def hidden(b, weights):
        @pl.loop(0, 4)
        def _(q):
            both = jnp.dot(xin[b], weights[q], preferred_element_type=F32)
            pre_gate, tan_gate = both[:144, :384], both[144:, :384]
            pre_up, tan_up = both[:144, 384:], both[144:, 384:]
            sigma = jax.nn.sigmoid(pre_gate)
            swish = pre_gate * sigma
            slope = sigma * (1.0 + pre_gate * (1.0 - sigma))
            lanes = pl.ds(pl.multiple_of(q * 384, 128), 384)
            hid[b, :144, lanes] = (swish * pre_up).astype(BF)
            hid[b, 144:, lanes] = (slope * tan_gate * pre_up + swish * tan_up).astype(BF)

    def own_half(b):
        for k in range(8 * b, 8 * b + 8):
            if k:
                token(k).wait_recv()
        here = rcv.at[128 * b : 128 * (b + 1)]
        unpack_tail(here, 8, tails)
        for kind in range(2):
            xin[b, 144 * kind : 144 * kind + 128] = here[:, 1280 * kind : 1280 * (kind + 1)]
            xin[b, 144 * kind + 128 : 144 * (kind + 1)] = tails[:, 1280 * kind : 1280 * (kind + 1)]
        hidden(b, gu_own)
        part[b] = jnp.dot(hid[b], dn_own[...], preferred_element_type=F32).astype(BF)

    arrive(1)
    pass_on(0)
    arrive(2)
    pass_on(1)
    finish(0)
    arrive(3)
    for copy in own:
        copy.wait()
    own_half(0)
    pass_on(2)
    finish(1)
    arrive(4)
    pass_on(3)
    finish(2)
    arrive(5)
    finish(3)
    for n in range(4):
        for i in range(4):
            over_core(n, i, 1 - c).wait_recv()
    hidden(0, gu_oth)
    pass_on(4)
    own_half(1)
    pass_on(5)
    finish(4)
    hidden(1, gu_oth)
    finish(5)
    for n in range(4, CHUNKS):
        for i in range(4):
            over_core(n, i, 1 - c).wait_recv()
    for b in (1, 0):
        here = jnp.dot(hid[b], dn_oth[...], preferred_element_type=F32).astype(BF)
        total = (here.astype(F32) + part[b].astype(F32)).astype(BF)
        back = rsend.at[128 * b : 128 * (b + 1)]
        for kind in range(2):
            back[:, 1280 * kind : 1280 * (kind + 1)] = total[144 * kind : 144 * kind + 128]
        pack_tail(jnp.concatenate([total[128:144], total[272:288]], 1), 8, back)
        for k in (15, 14, 13, 12, 11, 10, 9, 8) if b else (7, 6, 5, 4, 3, 2, 1):
            give_back(k).start()
    rback[:ROWS] = rsend[:ROWS]

    def combine(total, b, kind, width):
        lanes = slice(1280 * kind, 1280 * (kind + 1))
        for i in range(2):
            for rows, held in (
                (slice(128 * b, 128 * (b + 1)), rback[128 * b : 128 * (b + 1), lanes]),
                (slice(256 + 16 * b, 256 + 16 * (b + 1)), tails[:, lanes]),
            ):
                total += lax.dot_general(
                    wsel[i, rows, :width], held, (((0,), (0,)), ((), ())), preferred_element_type=F32
                )
        return total

    from_p, from_t = jnp.zeros((256, 1280), F32), jnp.zeros((128, 1280), F32)
    for b in (1, 0):
        for k in range(8 * b, 8 * b + 8):
            if k:
                give_back(k).wait_recv()
        unpack_tail(rback.at[128 * b : 128 * (b + 1)], 8, tails)
        from_p = combine(from_p, b, 0, 256)
        from_t = combine(from_t, b, 1, 128)
    out[:128] = from_p[:128].astype(BF)
    out[128:] = (from_t + from_p[128:]).astype(BF)

    for i in range(1, 8):
        for kind in range(2):
            regroup(i, kind).wait_send()
    for k in range(1, 16):
        token(k).wait_send()
        give_back(k).wait_send()
    for n in range(CHUNKS):
        cross(n).wait_send()
        for step in (1, -1):
            send_x(n, step).wait_send()
            send_on(n, step).wait_send()
        for i in range(4):
            over_core(n, i, c).wait_send()


def split(both, out_p, out_t):
    out_p[...] = both[:128]
    out_t[...] = both[128:]


def per_device(*args):
    args = [a.T for a in args[:5]] + list(args[5:])
    vmem, hbm = pl.BlockSpec(memory_space=pltpu.VMEM), pl.BlockSpec(memory_space=pl.ANY)
    dma = pltpu.SemaphoreType.DMA
    both = pl.pallas_call(
        layer,
        out_shape=jax.ShapeDtypeStruct((256, 1280), BF),
        in_specs=[hbm] * 2 + [vmem] * 3 + [hbm] * 3,
        out_specs=vmem,
        scratch_shapes=[
            pltpu.VMEM((2, 1280, 128), BF),
            pltpu.VMEM((256, LANES), BF),
            pltpu.VMEM((256, LANES), BF),
            pltpu.VMEM((256, LANES), BF),
            pltpu.VMEM((256, LANES), BF),
            pltpu.VMEM((4, 1280, 768), BF),
            pltpu.VMEM((1536, 1280), BF),
            pltpu.VMEM((4, 1280, 768), BF),
            pltpu.VMEM((1536, 1280), BF),
            pltpu.VMEM((2, 288, 1280), BF),
            pltpu.VMEM((2, 288, 1536), BF),
            pltpu.VMEM((2, 288, 1280), BF),
            pltpu.VMEM((16, 2560), BF),
            pltpu.VMEM((2, 288, 256), BF),
            dma((9,)),
            dma((2, 16)),
            dma((2, 16)),
            dma((2, 16)),
            dma((2, CHUNKS)),
            dma((2, 2 * CHUNKS)),
            dma((2, 2 * CHUNKS)),
            dma((2, 4 * CHUNKS)),
            pltpu.SemaphoreType.REGULAR,
        ],
        compiler_params=pltpu.CompilerParams(
            collective_id=0, has_side_effects=True, vmem_limit_bytes=60 << 20
        ),
    )(*args)
    return pl.pallas_call(split, out_shape=(jax.ShapeDtypeStruct((128, 1280), BF),) * 2)(both)


def solution(mesh):
    tokens = P(("exp", "seq"), None)
    halves = P("exp", None, None)
    return jax.shard_map(
        per_device,
        mesh=mesh,
        in_specs=(P("exp", "seq"), P("exp", "seq"), tokens, tokens, tokens, halves, halves, halves),
        out_specs=(tokens, tokens),
        check_vma=False,
    )
```

time: 145 us -> 117 us (0.81)
  Pallas kernels: 133 us -> 116 us
  local copies, waits for them, and re-layouts: 11.6 us -> 0 us
    pallas_call x1 -> x2, Pallas kernels: 133 us -> 116 us  [the longest x1 114 us: per_device(): pl.pallas_call(layer, out_shape=jax.ShapeDtypeStruct((256, 1280), BF), in...]
    unnamed x7 -> x0, local copies, waits for them, and re-layouts: 11.6 us -> none
where the time goes in v2:
time: 117 us
  Pallas kernels  116 us (99%)
    pallas_call x1, Pallas kernels, per_device(): pl.pallas_call(layer, out_shape=jax.ShapeDtypeStruct((256, 1280), BF), in...  114 us

profile of v2, /device:TPU:1, one launch (start us, length us, event | category | flops | bytes accessed | tf_op | source)
XLA Modules:
  0.0 117.0 jit_solution(11906491782095989649)
XLA Ops:
  0.6 114.4 %shard_map.95.both = bf16[256,1280]{1,0:T(8,128)(2,1)} custom-call(bf16[160,1024]{1,0:T(8,128)(2,1)} %bitcast.5, bf16[160,1024]{1,0:T(8,128)(2,1)} %bitcast.6, s32[2,128]{1,0:T(2,128)} %bitcast.7, f32[2,128]{1,0:T(2,128)} %bitcast.8, f32[2,128]{1,0:T(2,128)} %bitcast.9, bf16[1,1280,1536]{2,1,0:T(8,128)(2,1)} %w_gate.1, bf16[1,1280,1536]{2,1,0:T(8,128)(2,1)} %w_up.1, ...), custom_call_target="tpu_custom_call" | custom-call | tf_op jit(solution)/shard_map/pallas_call | solution.py:337
  115.1 1.9 %shard_map.96 = (bf16[128,1280]{1,0:T(8,128)(2,1)}, bf16[128,1280]{1,0:T(8,128)(2,1)}) custom-call(bf16[256,1280]{1,0:T(8,128)(2,1)} %shard_map.95.both), custom_call_target="tpu_custom_call" | custom-call | tf_op jit(solution)/shard_map/pallas_call | solution.py:371

commit v3 on v2

--- a/solution.py
+++ b/solution.py
@@ -190,21 +190,17 @@
             recv_on(n, step).wait_recv()
         over_core(n, 3, c).start()
 
-    arrive(0)
-    for kind in range(2):
-        regroup(0, kind).wait()
-        for i in range(1, 8):
-            regroup(i, kind).wait_recv()
+    def regrouped():
+        for kind in range(2):
+            regroup(0, kind).wait()
+            for i in range(1, 8):
+                regroup(i, kind).wait_recv()
 
     def dispatch(rows, kind):
         return lax.dot_general(
             rows, toks[kind], (((1,), (1,)), ((), ())), preferred_element_type=F32
         ).astype(BF)
 
-    for kind in range(2):
-        sbuf[:, 1280 * kind : 1280 * (kind + 1)] = dispatch(chosen[:256], kind)
-    pack_tail(jnp.concatenate([dispatch(chosen[256:], kind) for kind in range(2)], 1), 16, sbuf)
-
     def rows_of(k):
         return pl.ds(ROWS * k, ROWS)
 
@@ -214,16 +210,20 @@
     def give_back(k):
         return remote(rsend.at[rows_of(k)], rback.at[rows_of(k)], rt_sem.at[0, k], rt_sem.at[1, k], source(k))
 
-    pl.semaphore_wait(plane_sem, 3)
-    for first in (0, 2):
-        for j in range(4):
-            for d in (first + 1, first):
-                if d or j:
-                    token(4 * d + j).start()
-    rcv[:ROWS] = sbuf[:ROWS]
+    def send_rows():
+        for kind in range(2):
+            sbuf[:, 1280 * kind : 1280 * (kind + 1)] = dispatch(chosen[:256], kind)
+        pack_tail(jnp.concatenate([dispatch(chosen[256:], kind) for kind in range(2)], 1), 16, sbuf)
+        pl.semaphore_wait(plane_sem, 3)
+        for first in (0, 2):
+            for j in range(4):
+                for d in (first + 1, first):
+                    if d or j:
+                        token(4 * d + j).start()
+        rcv[:ROWS] = sbuf[:ROWS]
 
     def hidden(b, weights):
-        @pl.loop(0, 4)
+        @pl.loop(0, 4, unroll=2)
         def _(q):
             both = jnp.dot(xin[b], weights[q], preferred_element_type=F32)
             pre_gate, tan_gate = both[:144, :384], both[144:, :384]
@@ -235,7 +235,7 @@
             hid[b, :144, lanes] = (swish * pre_up).astype(BF)
             hid[b, 144:, lanes] = (slope * tan_gate * pre_up + swish * tan_up).astype(BF)
 
-    def own_half(b):
+    def rows_in(b):
         for k in range(8 * b, 8 * b + 8):
             if k:
                 token(k).wait_recv()
@@ -244,38 +244,34 @@
         for kind in range(2):
             xin[b, 144 * kind : 144 * kind + 128] = here[:, 1280 * kind : 1280 * (kind + 1)]
             xin[b, 144 * kind + 128 : 144 * (kind + 1)] = tails[:, 1280 * kind : 1280 * (kind + 1)]
+
+    def own_hidden(b):
         hidden(b, gu_own)
+
+    def own_down(b):
         part[b] = jnp.dot(hid[b], dn_own[...], preferred_element_type=F32).astype(BF)
 
-    arrive(1)
-    pass_on(0)
-    arrive(2)
-    pass_on(1)
-    finish(0)
-    arrive(3)
-    for copy in own:
-        copy.wait()
-    own_half(0)
-    pass_on(2)
-    finish(1)
-    arrive(4)
-    pass_on(3)
-    finish(2)
-    arrive(5)
-    finish(3)
-    for n in range(4):
+    def other_hidden(b):
+        hidden(b, gu_oth)
+
+    def own_here():
+        for copy in own:
+            copy.wait()
+
+    def from_core(n):
         for i in range(4):
             over_core(n, i, 1 - c).wait_recv()
-    hidden(0, gu_oth)
-    pass_on(4)
-    own_half(1)
-    pass_on(5)
-    finish(4)
-    hidden(1, gu_oth)
-    finish(5)
-    for n in range(4, CHUNKS):
-        for i in range(4):
-            over_core(n, i, 1 - c).wait_recv()
+
+    order = (
+        (arrive, 0), (regrouped,), (send_rows,), (arrive, 1), (pass_on, 0), (arrive, 2),
+        (pass_on, 1), (finish, 0), (arrive, 3), (pass_on, 2), (finish, 1), (own_here,),
+        (rows_in, 0), (own_hidden, 0), (arrive, 4), (pass_on, 3), (finish, 2), (own_down, 0),
+        (arrive, 5), (pass_on, 4), (finish, 3), (from_core, 0), (from_core, 1), (from_core, 2),
+        (from_core, 3), (other_hidden, 0), (rows_in, 1), (own_hidden, 1), (pass_on, 5), (finish, 4),
+        (own_down, 1), (other_hidden, 1), (finish, 5), (from_core, 4), (from_core, 5),
+    )
+    for step, *arg in order:
+        step(*arg)
     for b in (1, 0):
         here = jnp.dot(hid[b], dn_oth[...], preferred_element_type=F32).astype(BF)
         total = (here.astype(F32) + part[b].astype(F32)).astype(BF)
@@ -286,6 +282,19 @@
         for k in (15, 14, 13, 12, 11, 10, 9, 8) if b else (7, 6, 5, 4, 3, 2, 1):
             give_back(k).start()
     rback[:ROWS] = rsend[:ROWS]
+
+    for i in range(1, 8):
+        for kind in range(2):
+            regroup(i, kind).wait_send()
+    for k in range(1, 16):
+        token(k).wait_send()
+    for n in range(CHUNKS):
+        cross(n).wait_send()
+        for step in (1, -1):
+            send_x(n, step).wait_send()
+            send_on(n, step).wait_send()
+        for i in range(4):
+            over_core(n, i, c).wait_send()
 
     def combine(total, b, kind, width):
         lanes = slice(1280 * kind, 1280 * (kind + 1))
@@ -310,19 +319,8 @@
     out[:128] = from_p[:128].astype(BF)
     out[128:] = (from_t + from_p[128:]).astype(BF)
 
-    for i in range(1, 8):
-        for kind in range(2):
-            regroup(i, kind).wait_send()
     for k in range(1, 16):
-        token(k).wait_send()
         give_back(k).wait_send()
-    for n in range(CHUNKS):
-        cross(n).wait_send()
-        for step in (1, -1):
-            send_x(n, step).wait_send()
-            send_on(n, step).wait_send()
-        for i in range(4):
-            over_core(n, i, c).wait_send()
 
 
 def split(both, out_p, out_t):

time: 117 us -> 116 us (level)
    pallas_call x1, Pallas kernels: 114 us -> 113 us  [per_device(): pl.pallas_call(layer, out_shape=jax.ShapeDtypeStruct((256, 1280), BF), in...]
where the time goes in v3:
time: 116 us; the launch traced here: 115 us
  Pallas kernels  115 us (99%)
    pallas_call x1, Pallas kernels, per_device(): pl.pallas_call(layer, out_shape=jax.ShapeDtypeStruct((256, 1280), BF), in...  113 us

profile of v3, /device:TPU:1, one launch (start us, length us, event | category | flops | bytes accessed | tf_op | source)
XLA Modules:
  0.0 115.4 jit_solution(1680230331136343525)
XLA Ops:
  0.6 112.8 %shard_map.95.both = bf16[256,1280]{1,0:T(8,128)(2,1)} custom-call(bf16[160,1024]{1,0:T(8,128)(2,1)} %bitcast.5, bf16[160,1024]{1,0:T(8,128)(2,1)} %bitcast.6, s32[2,128]{1,0:T(2,128)} %bitcast.7, f32[2,128]{1,0:T(2,128)} %bitcast.8, f32[2,128]{1,0:T(2,128)} %bitcast.9, bf16[1,1280,1536]{2,1,0:T(8,128)(2,1)} %w_gate.1, bf16[1,1280,1536]{2,1,0:T(8,128)(2,1)} %w_up.1, ...), custom_call_target="tpu_custom_call" | custom-call | tf_op jit(solution)/shard_map/pallas_call | solution.py:335
  113.5 1.9 %shard_map.96 = (bf16[128,1280]{1,0:T(8,128)(2,1)}, bf16[128,1280]{1,0:T(8,128)(2,1)}) custom-call(bf16[256,1280]{1,0:T(8,128)(2,1)} %shard_map.95.both), custom_call_target="tpu_custom_call" | custom-call | tf_op jit(solution)/shard_map/pallas_call | solution.py:369

commit v4 on v3

--- a/solution.py
+++ b/solution.py
@@ -267,7 +267,7 @@
         (pass_on, 1), (finish, 0), (arrive, 3), (pass_on, 2), (finish, 1), (own_here,),
         (rows_in, 0), (own_hidden, 0), (arrive, 4), (pass_on, 3), (finish, 2), (own_down, 0),
         (arrive, 5), (pass_on, 4), (finish, 3), (from_core, 0), (from_core, 1), (from_core, 2),
-        (from_core, 3), (other_hidden, 0), (rows_in, 1), (own_hidden, 1), (pass_on, 5), (finish, 4),
+        (from_core, 3), (other_hidden, 0), (rows_in, 1), (pass_on, 5), (own_hidden, 1), (finish, 4),
         (own_down, 1), (other_hidden, 1), (finish, 5), (from_core, 4), (from_core, 5),
     )
     for step, *arg in order:

time: 116 us -> 115 us (level)
  no operation moved by 1% of the time
where the time goes in v4:
time: 115 us
  Pallas kernels  114 us (99%)
    pallas_call x1, Pallas kernels, per_device(): pl.pallas_call(layer, out_shape=jax.ShapeDtypeStruct((256, 1280), BF), in...  112 us

profile of v4, /device:TPU:1, one launch (start us, length us, event | category | flops | bytes accessed | tf_op | source)
XLA Modules:
  0.0 114.9 jit_solution(8042846854422936375)
XLA Ops:
  0.6 112.3 %shard_map.95.both = bf16[256,1280]{1,0:T(8,128)(2,1)} custom-call(bf16[160,1024]{1,0:T(8,128)(2,1)} %bitcast.5, bf16[160,1024]{1,0:T(8,128)(2,1)} %bitcast.6, s32[2,128]{1,0:T(2,128)} %bitcast.7, f32[2,128]{1,0:T(2,128)} %bitcast.8, f32[2,128]{1,0:T(2,128)} %bitcast.9, bf16[1,1280,1536]{2,1,0:T(8,128)(2,1)} %w_gate.1, bf16[1,1280,1536]{2,1,0:T(8,128)(2,1)} %w_up.1, ...), custom_call_target="tpu_custom_call" | custom-call | tf_op jit(solution)/shard_map/pallas_call | solution.py:335
  112.9 1.9 %shard_map.96 = (bf16[128,1280]{1,0:T(8,128)(2,1)}, bf16[128,1280]{1,0:T(8,128)(2,1)}) custom-call(bf16[256,1280]{1,0:T(8,128)(2,1)} %shard_map.95.both), custom_call_target="tpu_custom_call" | custom-call | tf_op jit(solution)/shard_map/pallas_call | solution.py:369
